TPU v7x, 512 devices: a whole 4x8x8 slice. The times are simulated.
512 devices in a mesh: ctx: 64 (over x, z, core), head: 8 (over y).
Axes of the slice: x: 4, y: 8, z: 8, core: 2. Of those that a mesh axis runs over, the one named last changes fastest.
Arguments:
- qkv: bfloat16 [1, 65536, 6144], P(None, ('ctx', 'head')), may hold values from -6 to 6
- grad_out: bfloat16 [1, 65536, 2048], P(None, ('ctx', 'head')), may hold values from -6 to 6
- w_qkv: bfloat16 [2048, 6144], P('ctx', 'head'), may hold values from -0.078125 to 0.078125
Outputs:
- grad_input: float32 [1, 65536, 2048], P(None, ('ctx', 'head'))
All inputs are finite; a program needn't handle non-finite values.
Results may differ from a plain program's by a relative error of at most 0.02.
Values may be sent and summed in bfloat16 or wider, within the bound.
A program may use at most 128 MiB of HBM per device.

v0:
```python
import math
import jax
import jax.numpy as jnp
from jax import lax
from jax.sharding import PartitionSpec as P

DH = 128


def carried_in(x, axis, join, neutral, backward):
    count = lax.axis_size(axis)
    place = lax.axis_index(axis)
    ahead = count - 1 - place if backward else place
    gathered = lax.all_gather(x.astype(jnp.bfloat16), axis)
    state = jnp.zeros_like(x) + jnp.asarray(neutral, x.dtype)

    def one(step, state):
        source = count - 1 - step if backward else step
        return join(state, lax.dynamic_index_in_dim(gathered, source, 0, False).astype(x.dtype))

    return lax.fori_loop(0, ahead, one, state)


def combine_sum(earlier, later):
    return earlier + later


def per_device(qkv, grad_out, w_qkv):
    highest = lax.Precision.HIGHEST
    whole_weight = lax.all_gather(w_qkv, "ctx", axis=0, tiled=True)
    local_qkv, local_grad = (
        lax.all_to_all(qkv, "head", split_axis=2, concat_axis=1, tiled=True),
        lax.all_to_all(grad_out, "head", split_axis=2, concat_axis=1, tiled=True),
    )
    num_seqs, block_len, width3 = local_qkv.shape
    heads_here = width3 // (3 * DH)
    factor = 1.0 / math.sqrt(DH * block_len * lax.axis_size("ctx"))
    blocks = local_qkv.reshape(num_seqs, block_len, heads_here, 3, DH)
    query_rows = blocks[:, :, :, 0]
    key_rows = blocks[:, :, :, 1]
    value_rows = blocks[:, :, :, 2]
    grad_rows = local_grad.reshape(num_seqs, block_len, heads_here, DH)
    kv_own = jnp.einsum("sthd,sthe->shde", key_rows, value_rows, preferred_element_type=jnp.float32)
    qg_own = jnp.einsum(
        "sthd,sthe->shde", query_rows, grad_rows, preferred_element_type=jnp.float32
    )
    empty_state = jnp.zeros_like(kv_own)
    kv_before = carried_in(kv_own, "ctx", combine_sum, empty_state, False)
    qg_after = carried_in(qg_own, "ctx", combine_sum, empty_state, True)
    positions = lax.broadcasted_iota(jnp.int32, (block_len, block_len), 0)
    columns = lax.broadcasted_iota(jnp.int32, (block_len, block_len), 1)
    causal = (positions >= columns).astype(jnp.float32)
    scores_gv = (
        jnp.einsum("sthe,suhe->shtu", grad_rows, value_rows, preferred_element_type=jnp.float32)
        * causal
    )
    scores_qk = (
        jnp.einsum("sthd,suhd->shtu", query_rows, key_rows, preferred_element_type=jnp.float32)
        * causal
    )
    key_wide = key_rows.astype(jnp.float32)
    grad_wide = grad_rows.astype(jnp.float32)
    grad_q = jnp.einsum("shtu,suhd->sthd", scores_gv, key_wide, precision=highest) + jnp.einsum(
        "sthe,shde->sthd", grad_wide, kv_before, precision=highest
    )
    query_wide = query_rows.astype(jnp.float32)
    value_wide = value_rows.astype(jnp.float32)
    grad_k = jnp.einsum("shtu,sthd->suhd", scores_gv, query_wide, precision=highest) + jnp.einsum(
        "suhe,shde->suhd", value_wide, qg_after, precision=highest
    )
    grad_v = jnp.einsum("shtu,sthe->suhe", scores_qk, grad_wide, precision=highest) + jnp.einsum(
        "suhd,shde->suhe", key_wide, qg_after, precision=highest
    )
    gradients = (
        (jnp.stack([grad_q, grad_k, grad_v], axis=3) * factor)
        .astype(jnp.bfloat16)
        .reshape(num_seqs, block_len, width3)
    )
    own_rows = lax.psum_scatter(
        jnp.einsum(
            "stf,df->tsd", gradients, whole_weight, preferred_element_type=jnp.float32
        ).astype(jnp.bfloat16),
        "head",
        scatter_dimension=0,
        tiled=True,
    ).astype(jnp.float32)
    return jnp.transpose(own_rows, (1, 0, 2))


def solution(mesh):
    in_specs = (P(None, ("ctx", "head"), None), P(None, ("ctx", "head"), None), P("ctx", "head"))
    out_specs = P(None, ("ctx", "head"), None)
    return jax.shard_map(
        per_device, mesh=mesh, in_specs=in_specs, out_specs=out_specs, check_vma=False
    )
```

profile of v0, /device:TPU:1, one launch (start us, length us, event | category | flops | bytes accessed | tf_op | source)
XLA Modules:
  0.0 456.7 jit_solution(5175588874633387678)
XLA Ops:
  6.5 2.3 copy.42
  9.4 11.4 %reduce = bf16[2048,128]{1,0:T(8,128)(2,1)S(1)} reduce(bf16[2048,1,128]{2,1,0:T(2,128)(2,1)S(1)} %bitcast.109, bf16[]{:T(256)} %broadcast.9), dimensions={1}, to_apply=%bitcast.91.reduce_sub_computation | reduce | bytes 1048578
  20.9 0.9 reshape.156
  21.8 7.7 %all-to-all-start = ((bf16[8,2,16384]{2,1,0:T(2,128)(2,1)}), bf16[8,2,16384]{2,1,0:T(2,128)(2,1)}, u32[]{:S(2)}, u32[]{:S(2)}) async-start(bf16[8,2,16384]{2,1,0:T(2,128)(2,1)} %reshape.156), calls=%async_computation | async-start | bytes 1048576 | tf_op jit(solution)/shard_map/all_to_all | solution.py:33
  29.4 6.8 %copy.44 = bf16[1,128,6144]{1,0,2:T(2,128)(2,1)S(1)} copy(bf16[1,128,6144]{2,1,0:T(8,128)(2,1)} %param.7) | data formatting | bytes 3145728 | tf_op args[0]
  36.2 34.3 %reduce.1 = bf16[6144,128]{1,0:T(8,128)(2,1)} reduce(bf16[6144,1,128]{2,1,0:T(2,128)(2,1)S(1)} %bitcast.105, bf16[]{:T(256)} %broadcast.9), dimensions={1}, to_apply=%bitcast.93.reduce_sub_computation | reduce | bytes 3145730
  70.6 3.7 reshape.158
  74.3 6.6 %all-to-all-start.1 = ((bf16[8,2,49152]{2,1,0:T(2,128)(2,1)}), bf16[8,2,49152]{2,1,0:T(2,128)(2,1)}, u32[]{:S(2)}, u32[]{:S(2)}) async-start(bf16[8,2,49152]{2,1,0:T(2,128)(2,1)} %reshape.158), calls=%async_computation.1 | async-start | bytes 3145728 | tf_op jit(solution)/shard_map/all_to_all | solution.py:32
  81.2 2.2 reshape.157
  83.8 1.0 reshape.144
  84.8 33.7 %all-to-all-done.1 = bf16[8,2,49152]{2,1,0:T(2,128)(2,1)} async-done(((bf16[8,2,49152]{2,1,0:T(2,128)(2,1)}), bf16[8,2,49152]{2,1,0:T(2,128)(2,1)}, u32[]{:S(2)}, u32[]{:S(2)}) %all-to-all-start.1) | async-done | bytes 1572896 | tf_op jit(solution)/shard_map/all_to_all | solution.py:32
  118.5 4.7 %reshape.159 = bf16[6144,1,128]{2,1,0:T(2,128)(2,1)S(1)} reshape(bf16[8,2,49152]{2,1,0:T(2,128)(2,1)} %all-to-all-done.1) | data formatting | bytes 3145728
  123.4 2.2 copy.45
  125.6 2.5 reshape.145
  128.2 0.9 convolution_convert_fusion
  129.2 0.9 convolution_convert_fusion.1
  131.4 4.5 fusion.24
  135.9 1.3 fusion.23
  137.2 4.3 fusion.14
  141.5 5.0 %fusion.11 = f32[2,128,1024]{2,1,0:T(8,128)S(1)} fusion(f32[2,1024,1024]{2,1,0:T(8,128)S(1)} %fusion.23, f32[1024,1024]{1,0:T(8,128)S(1)} %fusion.9, bf16[1,1024,2,3,128]{1,4,3,2,0:T(8,128)(2,1)S(1)} %reshape.145), kind=kOutput, calls=%fused_computation.16 | convolution fusion | flops 3223322624 | bytes 14155776 | tf_op jit(solution)/shard_map/shtu,suhd->sthd/dot_general | solution.py:63
  146.6 8.0 %fusion.17 = f32[2,128,1024]{2,1,0:T(8,128)} fusion(bf16[1024,2,128]{0,2,1:T(8,128)(2,1)S(1)} %copy-done, f32[2,1024,1024]{2,1,0:T(8,128)} %fusion.24, f32[1024,1024]{1,0:T(8,128)S(1)} %fusion.9), kind=kOutput, calls=%fused_computation.18 | convolution fusion | flops 3223322624 | bytes 14155776 | tf_op jit(solution)/shard_map/shtu,sthe->suhe/dot_general | solution.py:71
  154.6 62.5 %all-gather.10.cloned.1.call-done = bf16[128,128,128]{2,1,0:T(8,128)(2,1)} async-done(((bf16[2,128,128]{2,1,0:T(8,128)(2,1)}), bf16[128,128,128]{2,1,0:T(8,128)(2,1)}) %all-gather.10.cloned.1.call-update) | async-done | bytes 4194320 | tf_op jit(solution)/shard_map/all_gather | solution.py:14
  217.1 55.0 %while.23 = (s32[]{:T(128)}, f32[1,2,128,128]{3,2,1,0:T(8,128)S(1)}, s32[]{:T(128)}, bf16[64,1,2,128,128]{4,3,2,1,0:T(8,128)(2,1)}, s32[]{:T(128)}, /*index=5*/s32[]{:T(128)}, s32[]{:T(128)}, s32[]{:T(128)}) while((s32[]{:T(128)}, f32[1,2,128,128]{3,2,1,0:T(8,128)S(1)}, s32[]{:T(128)}, bf16[64,1,2,128,128]{4,3,2,1,0:T(8,128)(2,1)}, s32[]{:T(128)}, ...), condition=%wide.region_3.4_spmd, body=%wide.region_2.3_spmd.sunk | while | flops 65542 | bytes 327823 | solution.py:21
  220.6 0.9 convert_add_fusion.5
  221.5 0.9 convert_add_fusion.5
  229.5 0.9 convert_add_fusion.5
  230.4 0.9 convert_add_fusion.5
  231.3 0.9 convert_add_fusion.5
  232.2 0.9 convert_add_fusion.5
  237.5 0.9 convert_add_fusion.5
  241.0 0.9 convert_add_fusion.5
  247.2 0.9 convert_add_fusion.5
  248.1 0.9 convert_add_fusion.5
  249.0 0.9 convert_add_fusion.5
  253.5 0.9 convert_add_fusion.5
  254.3 0.9 convert_add_fusion.5
  261.4 0.9 convert_add_fusion.5
  262.3 0.9 convert_add_fusion.5
  270.3 0.9 convert_add_fusion.5
  271.2 0.9 convert_add_fusion.5
  272.1 2.9 fusion.20
  275.0 1.6 fusion.21
  276.6 25.6 %all-gather.8.cloned.1.call-done = bf16[128,128,128]{2,1,0:T(8,128)(2,1)} async-done(((bf16[2,128,128]{2,1,0:T(8,128)(2,1)}), bf16[128,128,128]{2,1,0:T(8,128)(2,1)}) %all-gather.8.cloned.1.call-update) | async-done | bytes 4194320 | tf_op jit(solution)/shard_map/all_gather | solution.py:14
  302.2 0.9 while.22
  304.9 81.9 %all-gather.6.cloned.1.call-done = bf16[2048,768]{1,0:T(8,128)(2,1)} async-done(((bf16[32,768]{1,0:T(8,128)(2,1)}), bf16[2048,768]{1,0:T(8,128)(2,1)}) %all-gather.6.cloned.1.call-update) | async-done | bytes 3145744 | tf_op jit(solution)/shard_map/all_gather | solution.py:30
  386.8 6.9 %convert_bitcast_fusion = bf16[1024,1,2048]{2,0,1:T(8,128)(2,1)} fusion(bf16[1024,768]{0,1:T(8,128)(2,1)S(1)} %bitcast.111, bf16[2048,768]{1,0:T(8,128)(2,1)} %all-gather.6.cloned.1.call-done), kind=kOutput, calls=%fused_computation.8 | convolution fusion | flops 3223322624 | bytes 8912896 | tf_op jit(solution)/shard_map/stf,df->tsd/dot_general | solution.py:80
  393.8 54.2 %reduce-scatter.2.cloned.1.call-done = bf16[128,1,2048]{2,0,1:T(8,128)(2,1)} async-done(((bf16[1024,1,2048]{2,0,1:T(8,128)(2,1)}), bf16[128,1,2048]{2,0,1:T(8,128)(2,1)}) %reduce-scatter.2.cloned.1.call-update) | async-done | bytes 524304 | tf_op jit(solution)/shard_map/reduce_scatter | solution.py:79
  448.0 2.1 bitcast_convert_fusion
  (73 shorter events, 44.2 us)
Async XLA Ops:
  21.8 52.5 %all-to-all-start = ((bf16[8,2,16384]{2,1,0:T(2,128)(2,1)}), bf16[8,2,16384]{2,1,0:T(2,128)(2,1)}, u32[]{:S(2)}, u32[]{:S(2)}) async-start(bf16[8,2,16384]{2,1,0:T(2,128)(2,1)} %reshape.156), calls=%async_computation | async-start | bytes 1048576 | tf_op jit(solution)/shard_map/all_to_all | solution.py:33
  74.3 44.2 %all-to-all-start.1 = ((bf16[8,2,49152]{2,1,0:T(2,128)(2,1)}), bf16[8,2,49152]{2,1,0:T(2,128)(2,1)}, u32[]{:S(2)}, u32[]{:S(2)}) async-start(bf16[8,2,49152]{2,1,0:T(2,128)(2,1)} %reshape.158), calls=%async_computation.1 | async-start | bytes 3145728 | tf_op jit(solution)/shard_map/all_to_all | solution.py:32
  80.9 136.1 %all-gather.10.cloned.1.call-start = ((), (), s32[]{:S(2)}) async-start(), calls=%async_computation.6 | async-start | bytes 4259840 | tf_op jit(solution)/shard_map/all_gather | solution.py:14
  123.4 4.7 %copy-start = (bf16[1024,2,128]{0,2,1:T(8,128)(2,1)S(1)}, bf16[1024,2,128]{0,2,1:T(8,128)(2,1)}, u32[]{:S(2)}) copy-start(bf16[1024,2,128]{0,2,1:T(8,128)(2,1)} %reshape.144) | copy-start | bytes 1572868
  129.1 173.1 %all-gather.8.cloned.1.call-start = ((), (), s32[]{:S(2)}) async-start(), calls=%async_computation.5 | async-start | bytes 4259840 | tf_op jit(solution)/shard_map/all_gather | solution.py:14
  130.1 256.7 %all-gather.6.cloned.1.call-start = ((), (), s32[]{:S(2)}) async-start(), calls=%async_computation.3 | async-start | bytes 3194880 | tf_op jit(solution)/shard_map/all_gather | solution.py:30
  130.8 317.2 %reduce-scatter.2.cloned.1.call-start = ((), (), s32[]{:S(2)}) async-start(), calls=%async_computation.4 | async-start | bytes 4718592 | tf_op jit(solution)/shard_map/reduce_scatter | solution.py:79
  272.1 2.9 copy-start.1
  276.6 27.2 %copy-start.2 = (f32[1,1024,2,1,128]{1,4,2,3,0:T(8,128)S(1)}, f32[1,1024,2,1,128]{1,4,2,3,0:T(8,128)}, u32[]{:S(2)}) copy-start(f32[1,1024,2,1,128]{1,4,2,3,0:T(8,128)} %fusion.20) | copy-start | bytes 3145732
  303.1 1.2 copy-start.3
Sparse Core Ops, SparseCore 0:
  129.2 87.7 all-gather.9
  220.4 81.7 all-gather.7
  305.6 81.2 all-gather.5
  393.9 54.0 reduce-scatter.1
where the time goes:
time: 460 us; the launch traced here: 457 us
  waiting for transfers between devices  259 us (56%)
  other arithmetic  103 us (22%)
  matrix products  37.1 us (8%)
  local copies, waits for them, and re-layouts  28.3 us (6%)
  starting transfers between devices  14.6 us (3%)
  between operations  13.3 us (3%)
    all_gather x2, waiting for transfers between devices, carried_in(): gathered = lax.all_gather(x.astype(jnp.bfloat16), axis)  88.1 us
    all_gather x1, waiting for transfers between devices, per_device(): whole_weight = lax.all_gather(w_qkv, 'ctx', axis=0, tiled=True)  81.9 us
    add x63, other arithmetic, combine_sum(): return earlier + later  54.4 us
    reduce_scatter x1, waiting for transfers between devices, per_device(): lax.psum_scatter(jnp.einsum('stf,df->tsd', gradients, whole_weight, prefe...  54.2 us
    unnamed x2, other arithmetic  45.8 us
    all_to_all x1, waiting for transfers between devices, per_device(): lax.all_to_all(qkv, 'head', split_axis=2, concat_axis=1, tiled=True)  33.7 us
    unnamed x17, local copies, waits for them, and re-layouts  22.1 us
  transfers between devices with their start and end apart: 6, of which 5 were waited for; matrix products, arithmetic and copies ran while one was open for 29% of the time, Pallas kernels for 0%

commit v1 on v0

--- a/solution.py
+++ b/solution.py
@@ -29,7 +29,10 @@
     highest = lax.Precision.HIGHEST
     whole_weight = lax.all_gather(w_qkv, "ctx", axis=0, tiled=True)
     local_qkv, local_grad = (
-        lax.all_to_all(qkv, "head", split_axis=2, concat_axis=1, tiled=True),
+        jnp.concatenate(
+            lax.all_to_all(jnp.stack(jnp.split(qkv, lax.axis_size("head"), axis=2)), "head", 0, 0),
+            axis=1,
+        ),
         lax.all_to_all(grad_out, "head", split_axis=2, concat_axis=1, tiled=True),
     )
     num_seqs, block_len, width3 = local_qkv.shape

time: 460 us -> 425 us (0.924)
  other arithmetic: 103 us -> 69 us
  waiting for transfers between devices: 259 us -> 275 us
  local copies, waits for them, and re-layouts: 28.3 us -> 19.3 us
  matrix products: 37.1 us -> 32.1 us
    unnamed x2 -> x1, other arithmetic: 45.8 us -> 11.5 us
    unnamed x17 -> x20, local copies, waits for them, and re-layouts: 22.1 us -> 13.1 us
    all_gather x2, waiting for transfers between devices: 88.1 us -> 95.9 us  [carried_in(): gathered = lax.all_gather(x.astype(jnp.bfloat16), axis)]
    all_to_all x1, waiting for transfers between devices: 0.01 us -> 6 us  [per_device(): lax.all_to_all(grad_out, 'head', split_axis=2, concat_axis=1, tiled=True)]
  transfers between devices with their start and end apart: 6 -> 6, of which waited for: 5 -> 6; matrix products, arithmetic and copies ran while one was open for 29% -> 21% of each run, Pallas kernels for 0% -> 0%
where the time goes in v1:
time: 425 us; the launch traced here: 422 us
  waiting for transfers between devices  275 us (65%)
  other arithmetic  69 us (16%)
  matrix products  32.1 us (8%)
  local copies, waits for them, and re-layouts  19.3 us (5%)
  between operations  13.3 us (3%)
  starting transfers between devices  11.6 us (3%)
    all_gather x2, waiting for transfers between devices, carried_in(): gathered = lax.all_gather(x.astype(jnp.bfloat16), axis)  95.9 us
    all_gather x1, waiting for transfers between devices, per_device(): whole_weight = lax.all_gather(w_qkv, 'ctx', axis=0, tiled=True)  81.6 us
    add x63, other arithmetic, combine_sum(): return earlier + later  54.5 us
    reduce_scatter x1, waiting for transfers between devices, per_device(): lax.psum_scatter(jnp.einsum('stf,df->tsd', gradients, whole_weight, prefe...  54.2 us
    all_to_all x1, waiting for transfers between devices, per_device(): lax.all_to_all(jnp.stack(jnp.split(qkv, lax.axis_size('head'), axis=2)),...  36.3 us
    unnamed x20, local copies, waits for them, and re-layouts  13.1 us
    unnamed x1, other arithmetic  11.5 us
  transfers between devices with their start and end apart: 6, of which 6 were waited for; matrix products, arithmetic and copies ran while one was open for 21% of the time, Pallas kernels for 0%

profile of v1, /device:TPU:1, one launch (start us, length us, event | category | flops | bytes accessed | tf_op | source)
XLA Modules:
  0.0 421.5 jit_solution(8330790206316403219)
XLA Ops:
  6.5 2.3 copy.54
  9.4 11.5 %reduce = bf16[2048,128]{1,0:T(8,128)(2,1)S(1)} reduce(bf16[2048,1,128]{2,1,0:T(2,128)(2,1)S(1)} %bitcast.117, bf16[]{:T(256)} %broadcast.9), dimensions={1}, to_apply=%bitcast.104.reduce_sub_computation | reduce | bytes 1048578
  20.9 0.9 reshape.147
  21.8 7.7 %all-to-all-start.1 = ((bf16[8,2,16384]{2,1,0:T(2,128)(2,1)}), bf16[8,2,16384]{2,1,0:T(2,128)(2,1)S(1)}, u32[]{:S(2)}, u32[]{:S(2)}) async-start(bf16[8,2,16384]{2,1,0:T(2,128)(2,1)} %reshape.147), calls=%async_computation.1 | async-start | bytes 1048576 | tf_op jit(solution)/shard_map/all_to_all | solution.py:36
  29.5 0.9 bitcast_dynamic-update-slice_fusion.7
  30.4 0.9 bitcast_dynamic-update-slice_fusion.6
  31.4 0.9 bitcast_dynamic-update-slice_fusion.5
  32.3 0.9 bitcast_dynamic-update-slice_fusion.4
  33.3 0.9 bitcast_dynamic-update-slice_fusion.3
  34.2 0.9 bitcast_dynamic-update-slice_fusion.2
  35.2 0.9 bitcast_dynamic-update-slice_fusion.1
  36.1 0.9 bitcast_dynamic-update-slice_fusion
  37.1 1.2 copy-done.3
  38.2 6.0 %all-to-all-done.1 = bf16[8,2,16384]{2,1,0:T(2,128)(2,1)S(1)} async-done(((bf16[8,2,16384]{2,1,0:T(2,128)(2,1)}), bf16[8,2,16384]{2,1,0:T(2,128)(2,1)S(1)}, u32[]{:S(2)}, u32[]{:S(2)}) %all-to-all-start.1) | async-done | bytes 524320 | tf_op jit(solution)/shard_map/all_to_all | solution.py:36
  44.2 3.6 all-to-all-start
  49.1 36.3 %all-to-all-done = bf16[8,1,128,768]{3,2,1,0:T(8,128)(2,1)S(1)} async-done(((bf16[8,1,128,768]{3,2,1,0:T(8,128)(2,1)}), bf16[8,1,128,768]{3,2,1,0:T(8,128)(2,1)S(1)}, u32[]{:S(2)}, u32[]{:S(2)}) %all-to-all-start) | async-done | bytes 1572896 | tf_op jit(solution)/shard_map/all_to_all | solution.py:33
  85.4 2.0 copy.51
  87.4 2.5 reshape_reshape.3
  89.9 0.9 convolution_convert_fusion
  91.0 0.9 convolution_convert_fusion.1
  93.4 1.3 fusion.16
  94.7 1.3 fusion.15
  96.0 6.0 %fusion.2 = f32[2,128,1024]{2,1,0:T(8,128)} fusion(f32[2,1024,1024]{2,1,0:T(8,128)S(1)} %fusion.15, f32[1024,1024]{0,1:T(8,128)S(1)} %fusion.7, bf16[1,1024,2,3,128]{1,4,3,2,0:T(8,128)(2,1)S(1)} %reshape_reshape.3), kind=kOutput, calls=%fused_computation.5 | convolution fusion | flops 3223322624 | bytes 14155776 | tf_op jit(solution)/shard_map/shtu,sthd->suhd/dot_general | solution.py:71
  102.0 3.4 fusion.3
  105.4 6.2 %fusion.9 = f32[2,128,1024]{2,1,0:T(8,128)} fusion(bf16[1024,2,128]{0,2,1:T(8,128)(2,1)S(1)} %reshape.138, f32[2,1024,1024]{1,2,0:T(8,128)S(1)} %fusion.16, f32[1024,1024]{0,1:T(8,128)S(1)} %fusion.7), kind=kOutput, calls=%fused_computation.15 | convolution fusion | flops 3223322624 | bytes 14155776 | tf_op jit(solution)/shard_map/shtu,sthe->suhe/dot_general | solution.py:74
  111.6 70.3 %all-gather.10.cloned.1.call-done = bf16[128,128,128]{2,1,0:T(8,128)(2,1)} async-done(((bf16[2,128,128]{2,1,0:T(8,128)(2,1)}), bf16[128,128,128]{2,1,0:T(8,128)(2,1)}) %all-gather.10.cloned.1.call-update) | async-done | bytes 4194320 | tf_op jit(solution)/shard_map/all_gather | solution.py:14
  181.9 55.0 %while.23 = (s32[]{:T(128)}, f32[1,2,128,128]{3,2,1,0:T(8,128)S(1)}, s32[]{:T(128)}, bf16[64,1,2,128,128]{4,3,2,1,0:T(8,128)(2,1)}, s32[]{:T(128)}, /*index=5*/s32[]{:T(128)}, s32[]{:T(128)}, s32[]{:T(128)}) while((s32[]{:T(128)}, f32[1,2,128,128]{3,2,1,0:T(8,128)S(1)}, s32[]{:T(128)}, bf16[64,1,2,128,128]{4,3,2,1,0:T(8,128)(2,1)}, s32[]{:T(128)}, ...), condition=%wide.region_3.4_spmd, body=%wide.region_2.3_spmd.sunk | while | flops 65542 | bytes 327823 | solution.py:21
  181.9 0.9 convert_add_fusion.5
  182.8 0.9 convert_add_fusion.5
  183.7 0.9 convert_add_fusion.5
  184.6 0.9 convert_add_fusion.5
  185.5 0.9 convert_add_fusion.5
  189.9 0.9 convert_add_fusion.5
  195.2 0.9 convert_add_fusion.5
  196.1 0.9 convert_add_fusion.5
  197.0 0.9 convert_add_fusion.5
  202.3 0.9 convert_add_fusion.5
  205.9 0.9 convert_add_fusion.5
  213.9 0.9 convert_add_fusion.5
  236.0 0.9 convert_add_fusion.5
  236.9 2.9 fusion.12
  239.9 1.6 fusion.13
  241.4 25.7 %all-gather.8.cloned.1.call-done = bf16[128,128,128]{2,1,0:T(8,128)(2,1)} async-done(((bf16[2,128,128]{2,1,0:T(8,128)(2,1)}), bf16[128,128,128]{2,1,0:T(8,128)(2,1)}) %all-gather.8.cloned.1.call-update) | async-done | bytes 4194320 | tf_op jit(solution)/shard_map/all_gather | solution.py:14
  267.1 0.9 while.22
  270.1 81.6 %all-gather.6.cloned.1.call-done = bf16[2048,768]{1,0:T(8,128)(2,1)} async-done(((bf16[32,768]{1,0:T(8,128)(2,1)}), bf16[2048,768]{1,0:T(8,128)(2,1)}) %all-gather.6.cloned.1.call-update) | async-done | bytes 3145744 | tf_op jit(solution)/shard_map/all_gather | solution.py:30
  351.7 7.0 %convert_bitcast_fusion = bf16[1024,1,2048]{2,0,1:T(8,128)(2,1)} fusion(bf16[1024,768]{0,1:T(8,128)(2,1)S(1)} %bitcast.119, bf16[2048,768]{1,0:T(8,128)(2,1)} %all-gather.6.cloned.1.call-done), kind=kOutput, calls=%fused_computation.7 | convolution fusion | flops 3223322624 | bytes 8912896 | tf_op jit(solution)/shard_map/stf,df->tsd/dot_general | solution.py:83
  358.7 54.2 %reduce-scatter.2.cloned.1.call-done = bf16[128,1,2048]{2,0,1:T(8,128)(2,1)} async-done(((bf16[1024,1,2048]{2,0,1:T(8,128)(2,1)}), bf16[128,1,2048]{2,0,1:T(8,128)(2,1)}) %reduce-scatter.2.cloned.1.call-update) | async-done | bytes 524304 | tf_op jit(solution)/shard_map/reduce_scatter | solution.py:82
  412.9 2.1 bitcast_convert_fusion
  (76 shorter events, 48.6 us)
Async XLA Ops:
  21.8 22.4 %all-to-all-start.1 = ((bf16[8,2,16384]{2,1,0:T(2,128)(2,1)}), bf16[8,2,16384]{2,1,0:T(2,128)(2,1)S(1)}, u32[]{:S(2)}, u32[]{:S(2)}) async-start(bf16[8,2,16384]{2,1,0:T(2,128)(2,1)} %reshape.147), calls=%async_computation.1 | async-start | bytes 1048576 | tf_op jit(solution)/shard_map/all_to_all | solution.py:36
  37.1 1.2 copy-start.3
  44.2 41.1 %all-to-all-start = ((bf16[8,1,128,768]{3,2,1,0:T(8,128)(2,1)}), bf16[8,1,128,768]{3,2,1,0:T(8,128)(2,1)S(1)}, u32[]{:S(2)}, u32[]{:S(2)}) async-start(bf16[8,1,128,768]{3,2,1,0:T(8,128)(2,1)} %copy-done.3), calls=%async_computation | async-start | bytes 3145728 | tf_op jit(solution)/shard_map/all_to_all | solution.py:33
  47.8 134.1 %all-gather.10.cloned.1.call-start = ((), (), s32[]{:S(2)}) async-start(), calls=%async_computation.6 | async-start | bytes 4259840 | tf_op jit(solution)/shard_map/all_gather | solution.py:14
  90.9 176.2 %all-gather.8.cloned.1.call-start = ((), (), s32[]{:S(2)}) async-start(), calls=%async_computation.5 | async-start | bytes 4259840 | tf_op jit(solution)/shard_map/all_gather | solution.py:14
  91.9 259.8 %all-gather.6.cloned.1.call-start = ((), (), s32[]{:S(2)}) async-start(), calls=%async_computation.3 | async-start | bytes 3194880 | tf_op jit(solution)/shard_map/all_gather | solution.py:30
  92.6 320.3 %reduce-scatter.2.cloned.1.call-start = ((), (), s32[]{:S(2)}) async-start(), calls=%async_computation.4 | async-start | bytes 4718592 | tf_op jit(solution)/shard_map/reduce_scatter | solution.py:82
  236.9 2.9 copy-start
  268.0 1.2 copy-start.1
  268.0 1.5 copy-start.2
Sparse Core Ops, SparseCore 0:
  91.0 90.8 all-gather.9
  185.3 81.7 all-gather.7
  270.4 81.2 all-gather.5
  358.8 54.0 reduce-scatter.1
